TPU v7x, 32 devices: a whole 2x2x4 slice. The times are simulated.
32 devices in a mesh: grp: 8 (over z, x), seq: 4 (over y, core).
Axes of the slice: x: 2, y: 2, z: 4, core: 2. Of those that a mesh axis runs over, the one named last changes fastest.
Arguments:
- tokens: bfloat16 [16, 448, 768], P('grp', 'seq'), may hold values from -6 to 6
- encoder_states: bfloat16 [16, 1500, 768], P('grp', 'seq'), may hold values from -6 to 6
- lengths: int32 [16], P('grp'), may hold values from 56 to 448, as said below
- frame_counts: int32 [16], P('grp'), may hold values from 375 to 1500, as said below
- corpus_ids: int32 [16], P('grp'), may hold values from 0 to 8
- corpus_weights: float32 [9], replicated, may hold values from 0.5 to 2
- cotangent: bfloat16 [16, 448, 768], P('grp', 'seq'), may hold values from -6 to 6
- first_gain: bfloat16 [768], P('grp'), may hold values from 0.5 to 1.5
- first_bias: bfloat16 [768], P('grp'), may hold values from -1.5 to 1.5
- query_weight: bfloat16 [768, 768], P('grp', 'seq'), may hold values from -0.3125 to 0.3125
- query_bias: bfloat16 [768], P('grp'), may hold values from -1.5 to 1.5
- key_weight: bfloat16 [768, 768], P('grp', 'seq'), may hold values from -0.3125 to 0.3125
- value_weight: bfloat16 [768, 768], P('grp', 'seq'), may hold values from -0.21875 to 0.21875
- value_bias: bfloat16 [768], P('grp'), may hold values from -1.5 to 1.5
- output_weight: bfloat16 [768, 768], P('grp', 'seq'), may hold values from -1.75 to 1.75
- output_bias: bfloat16 [768], P('grp'), may hold values from -1.5 to 1.5
- second_gain: bfloat16 [768], P('grp'), may hold values from 0.5 to 1.5
- second_bias: bfloat16 [768], P('grp'), may hold values from -1.5 to 1.5
- cross_query_weight: bfloat16 [768, 768], P('grp', 'seq'), may hold values from -0.3125 to 0.3125
- cross_query_bias: bfloat16 [768], P('grp'), may hold values from -1.5 to 1.5
- cross_key_weight: bfloat16 [768, 768], P('grp', 'seq'), may hold values from -0.3125 to 0.3125
- cross_value_weight: bfloat16 [768, 768], P('grp', 'seq'), may hold values from -0.21875 to 0.21875
- cross_value_bias: bfloat16 [768], P('grp'), may hold values from -1.5 to 1.5
- cross_output_weight: bfloat16 [768, 768], P('grp', 'seq'), may hold values from -2.5 to 2.5
- cross_output_bias: bfloat16 [768], P('grp'), may hold values from -1.5 to 1.5
- third_gain: bfloat16 [768], P('grp'), may hold values from 0.5 to 1.5
- third_bias: bfloat16 [768], P('grp'), may hold values from -1.5 to 1.5
- expand_weight: bfloat16 [768, 3072], P('grp', 'seq'), may hold values from -0.21875 to 0.21875
- expand_bias: bfloat16 [3072], P('grp'), may hold values from -1.5 to 1.5
- reduce_weight: bfloat16 [3072, 768], P('grp', 'seq'), may hold values from -0.109375 to 0.109375
- reduce_bias: bfloat16 [768], P('grp'), may hold values from -1.5 to 1.5
Outputs:
- layer_output: bfloat16 [16, 448, 768], P('grp', 'seq')
- tokens_gradient: bfloat16 [16, 448, 768], P('grp', 'seq')
- first_gain_gradient: float32 [768], P('grp')
- first_bias_gradient: float32 [768], P('grp')
- query_weight_gradient: float32 [768, 768], P('grp', 'seq')
- query_bias_gradient: float32 [768], P('grp')
- key_weight_gradient: float32 [768, 768], P('grp', 'seq')
- value_weight_gradient: float32 [768, 768], P('grp', 'seq')
- value_bias_gradient: float32 [768], P('grp')
- output_weight_gradient: float32 [768, 768], P('grp', 'seq')
- output_bias_gradient: float32 [768], P('grp')
- second_gain_gradient: float32 [768], P('grp')
- second_bias_gradient: float32 [768], P('grp')
- cross_query_weight_gradient: float32 [768, 768], P('grp', 'seq')
- cross_query_bias_gradient: float32 [768], P('grp')
- cross_key_weight_gradient: float32 [768, 768], P('grp', 'seq')
- cross_value_weight_gradient: float32 [768, 768], P('grp', 'seq')
- cross_value_bias_gradient: float32 [768], P('grp')
- cross_output_weight_gradient: float32 [768, 768], P('grp', 'seq')
- cross_output_bias_gradient: float32 [768], P('grp')
- third_gain_gradient: float32 [768], P('grp')
- third_bias_gradient: float32 [768], P('grp')
- expand_weight_gradient: float32 [768, 3072], P('grp', 'seq')
- expand_bias_gradient: float32 [3072], P('grp')
- reduce_weight_gradient: float32 [3072, 768], P('grp', 'seq')
- reduce_bias_gradient: float32 [768], P('grp')
Inputs may be any that keep to these rules, and one draw needn't show every extreme that they name: `lengths`: in each aligned block of 2 transcripts one has more than 336 valid tokens; some transcript has exactly 448. `frame_counts`: in each aligned block of 2 clips one has more than 1125 valid frames; some clip has exactly 1500.
All inputs are finite; a program needn't handle non-finite values.
Results may differ from a plain program's by a relative error of at most 0.025.
Values may be sent and summed in bfloat16 or wider, within the bound.
A program may use at most 192 MiB of HBM per device.

v0:
```python
import math

import jax
import jax.numpy as jnp
from jax import lax
from jax.sharding import PartitionSpec as P

HEADS = 12
HEAD_DIM = 64


NEG = -1e30
EPS = 1e-05


def norm_rows(values, scaling, offset):
    centre = values - jnp.mean(values, axis=-1, keepdims=True)
    spread = jnp.mean(centre * centre, axis=-1, keepdims=True)
    return centre * lax.rsqrt(spread + EPS) * scaling + offset


def smooth_gate(values):
    return 0.5 * values * (1.0 + lax.erf(values * 0.7071067811865476))


def linear(inputs, weight):
    return jnp.einsum("bri,ij->brj", inputs, weight, preferred_element_type=jnp.float32)


def linear_back(gradient, weight):
    return jnp.einsum("brj,ij->bri", gradient, weight, preferred_element_type=jnp.float32)


def outer_sum(inputs, gradient):
    return jnp.einsum("bri,brj->ij", inputs, gradient, preferred_element_type=jnp.float32)


def row_total(gradient):
    return jnp.sum(gradient.astype(jnp.float32), axis=(0, 1))


def split_heads(values):
    return values.reshape(values.shape[0], values.shape[1], HEADS, HEAD_DIM)


def scores_of(query, key_rows, allowed):
    scores = jnp.einsum(
        "bqhd,bkhd->bhqk",
        split_heads(query),
        split_heads(key_rows),
        preferred_element_type=jnp.float32,
    )
    return jnp.where(allowed[:, None], scores, NEG)


def attend(query, key_rows, values, allowed):
    scores = scores_of(query, key_rows, allowed)
    maximum = jnp.max(scores, axis=-1, keepdims=True)
    raised = jnp.exp(scores - maximum)
    summed = jnp.sum(raised, axis=-1, keepdims=True)
    chances = (raised / summed).astype(jnp.bfloat16)
    blended = jnp.einsum(
        "bhqk,bkhd->bqhd", chances, split_heads(values), preferred_element_type=jnp.float32
    )
    return (blended.reshape(query.shape).astype(jnp.bfloat16), maximum + jnp.log(summed))


def attend_back(grad_low, query, key_rows, values, allowed, logsum):
    scores = scores_of(query, key_rows, allowed)
    chances = jnp.exp(scores - logsum)
    grad_heads = split_heads(grad_low)
    grad_chance = jnp.einsum(
        "bqhd,bkhd->bhqk", grad_heads, split_heads(values), preferred_element_type=jnp.float32
    )
    offset = jnp.sum(chances * grad_chance, axis=-1, keepdims=True)
    grad_score = (chances * (grad_chance - offset)).astype(jnp.bfloat16)
    grad_query = jnp.einsum(
        "bhqk,bkhd->bqhd", grad_score, split_heads(key_rows), preferred_element_type=jnp.float32
    )
    grad_keys = jnp.einsum(
        "bhqk,bqhd->bkhd", grad_score, split_heads(query), preferred_element_type=jnp.float32
    )
    grad_values = jnp.einsum(
        "bhqk,bqhd->bkhd",
        chances.astype(jnp.bfloat16),
        grad_heads,
        preferred_element_type=jnp.float32,
    )
    return (
        grad_query.reshape(query.shape),
        grad_keys.reshape(key_rows.shape),
        grad_values.reshape(values.shape),
    )


def on_device(
    tokens,
    encoder_states,
    lengths,
    frame_counts,
    corpus_ids,
    corpus_weights,
    cotangent,
    first_gain,
    first_bias,
    query_weight,
    query_bias,
    key_weight,
    value_weight,
    value_bias,
    output_weight,
    output_bias,
    second_gain,
    second_bias,
    cross_query_weight,
    cross_query_bias,
    cross_key_weight,
    cross_value_weight,
    cross_value_bias,
    cross_output_weight,
    cross_output_bias,
    third_gain,
    third_bias,
    expand_weight,
    expand_bias,
    reduce_weight,
    reduce_bias,
):
    row_parts = (
        lax.all_gather(query_weight, "grp", axis=0, tiled=True),
        lax.all_gather(key_weight, "grp", axis=0, tiled=True),
        lax.all_gather(value_weight, "grp", axis=0, tiled=True),
        lax.all_gather(output_weight, "grp", axis=0, tiled=True),
        lax.all_gather(cross_query_weight, "grp", axis=0, tiled=True),
        lax.all_gather(cross_key_weight, "grp", axis=0, tiled=True),
        lax.all_gather(cross_value_weight, "grp", axis=0, tiled=True),
        lax.all_gather(cross_output_weight, "grp", axis=0, tiled=True),
        lax.all_gather(expand_weight, "grp", axis=0, tiled=True),
        lax.all_gather(reduce_weight, "grp", axis=0, tiled=True),
        lax.all_gather(first_gain, "grp", axis=0, tiled=True),
        lax.all_gather(first_bias, "grp", axis=0, tiled=True),
        lax.all_gather(query_bias, "grp", axis=0, tiled=True),
        lax.all_gather(value_bias, "grp", axis=0, tiled=True),
        lax.all_gather(output_bias, "grp", axis=0, tiled=True),
        lax.all_gather(second_gain, "grp", axis=0, tiled=True),
        lax.all_gather(second_bias, "grp", axis=0, tiled=True),
        lax.all_gather(cross_query_bias, "grp", axis=0, tiled=True),
        lax.all_gather(cross_value_bias, "grp", axis=0, tiled=True),
        lax.all_gather(cross_output_bias, "grp", axis=0, tiled=True),
        lax.all_gather(third_gain, "grp", axis=0, tiled=True),
        lax.all_gather(third_bias, "grp", axis=0, tiled=True),
        lax.all_gather(expand_bias, "grp", axis=0, tiled=True),
        lax.all_gather(reduce_bias, "grp", axis=0, tiled=True),
    )
    gathered = (
        lax.all_gather(row_parts[0], "seq", axis=1, tiled=True),
        lax.all_gather(row_parts[1], "seq", axis=1, tiled=True),
        lax.all_gather(row_parts[2], "seq", axis=1, tiled=True),
        lax.all_gather(row_parts[3], "seq", axis=1, tiled=True),
        lax.all_gather(row_parts[4], "seq", axis=1, tiled=True),
        lax.all_gather(row_parts[5], "seq", axis=1, tiled=True),
        lax.all_gather(row_parts[6], "seq", axis=1, tiled=True),
        lax.all_gather(row_parts[7], "seq", axis=1, tiled=True),
        lax.all_gather(row_parts[8], "seq", axis=1, tiled=True),
        lax.all_gather(row_parts[9], "seq", axis=1, tiled=True),
    )
    w_query, w_key, w_value, w_mixer, x_query, x_key, x_value, x_mixer, w_expand, w_reduce = (
        gathered
    )
    vectors = [piece.astype(jnp.float32) for piece in row_parts[10:]]
    factor = 1.0 / math.sqrt(HEAD_DIM)
    seq_count = lax.axis_size("seq")
    span_rows = tokens.shape[1]
    query_pos = lax.axis_index("seq") * span_rows + jnp.arange(span_rows, dtype=jnp.int32)
    key_pos = jnp.arange(span_rows * seq_count, dtype=jnp.int32)
    self_mask = (key_pos[None, None, :] <= query_pos[None, :, None]) & (
        key_pos[None, None, :] < lengths[:, None, None]
    )
    frame_pos = jnp.arange(encoder_states.shape[1] * seq_count, dtype=jnp.int32)
    cross_mask = frame_pos[None, None, :] < frame_counts[:, None, None]
    layer_in = tokens.astype(jnp.float32)
    normed_one, norm_back_one = jax.vjp(norm_rows, layer_in, vectors[0], vectors[1])
    normed_one = normed_one.astype(jnp.bfloat16)
    query_low = ((linear(normed_one, w_query) + vectors[2]) * factor).astype(jnp.bfloat16)
    key_low = linear(normed_one, w_key).astype(jnp.bfloat16)
    value_low = (linear(normed_one, w_value) + vectors[3]).astype(jnp.bfloat16)
    key_all, value_all = (
        lax.all_gather(key_low, "seq", axis=1, tiled=True),
        lax.all_gather(value_low, "seq", axis=1, tiled=True),
    )
    self_out, self_logsum = attend(query_low, key_all, value_all, self_mask)
    after_self = layer_in + linear(self_out, w_mixer) + vectors[4]
    normed_two, norm_back_two = jax.vjp(norm_rows, after_self, vectors[5], vectors[6])
    normed_two = normed_two.astype(jnp.bfloat16)
    cross_query = ((linear(normed_two, x_query) + vectors[7]) * factor).astype(jnp.bfloat16)
    frames_all = lax.all_gather(encoder_states, "seq", axis=1, tiled=True)
    cross_keys_all = linear(frames_all, x_key).astype(jnp.bfloat16)
    cross_values_all = (linear(frames_all, x_value) + vectors[8]).astype(jnp.bfloat16)
    cross_out, cross_logsum = attend(cross_query, cross_keys_all, cross_values_all, cross_mask)
    after_cross = after_self + linear(cross_out, x_mixer) + vectors[9]
    normed_three, norm_back_three = jax.vjp(norm_rows, after_cross, vectors[10], vectors[11])
    normed_three = normed_three.astype(jnp.bfloat16)
    hidden = linear(normed_three, w_expand) + vectors[12]
    gated, gate_back = jax.vjp(smooth_gate, hidden)
    gated_low = gated.astype(jnp.bfloat16)
    result = after_cross + linear(gated_low, w_reduce) + vectors[13]
    layer_output = result.astype(jnp.bfloat16)
    present = (query_pos[None, :] < lengths[:, None]).astype(jnp.float32)
    corpus_index = jnp.arange(corpus_weights.shape[0], dtype=jnp.int32)
    corpus_scale = jnp.sum(
        jnp.where(corpus_ids[:, None] == corpus_index[None, :], corpus_weights[None, :], 0.0),
        axis=1,
    )
    grad_out = cotangent.astype(jnp.float32) * (present * corpus_scale[:, None])[:, :, None]
    reduce_low = grad_out.astype(jnp.bfloat16)
    slope_reduce_bias = row_total(reduce_low)
    slope_reduce = outer_sum(gated_low, reduce_low)
    grad_hidden = gate_back(linear_back(reduce_low, w_reduce))[0]
    hidden_low = grad_hidden.astype(jnp.bfloat16)
    slope_expand_bias = row_total(hidden_low)
    slope_expand = outer_sum(normed_three, hidden_low)
    grad_norm_in, slope_gain_three, slope_bias_three = norm_back_three(
        linear_back(hidden_low, w_expand)
    )
    grad_cross = grad_out + grad_norm_in
    cross_low = grad_cross.astype(jnp.bfloat16)
    slope_xmixer_bias = row_total(cross_low)
    slope_xmixer = outer_sum(cross_out, cross_low)
    grad_heard = linear_back(cross_low, x_mixer).astype(jnp.bfloat16)
    grad_cq, part_ck, part_cv = attend_back(
        grad_heard, cross_query, cross_keys_all, cross_values_all, cross_mask, cross_logsum
    )
    slope_xkey = outer_sum(frames_all, part_ck)
    slope_xvalue = outer_sum(frames_all, part_cv)
    slope_xvalue_bias = row_total(part_cv)
    low_cq = (grad_cq * factor).astype(jnp.bfloat16)
    slope_xquery_bias = row_total(low_cq)
    slope_xquery = outer_sum(normed_two, low_cq)
    grad_norm_two, slope_gain_two, slope_bias_two = norm_back_two(linear_back(low_cq, x_query))
    grad_self = grad_cross + grad_norm_two
    self_low = grad_self.astype(jnp.bfloat16)
    slope_mixer_bias = row_total(self_low)
    slope_mixer = outer_sum(self_out, self_low)
    grad_mixed = linear_back(self_low, w_mixer).astype(jnp.bfloat16)
    grad_q, part_k, part_v = attend_back(
        grad_mixed, query_low, key_all, value_all, self_mask, self_logsum
    )
    summed_k, summed_v = (
        lax.psum_scatter(
            part_k.astype(jnp.bfloat16), "seq", scatter_dimension=1, tiled=True
        ).astype(jnp.float32),
        lax.psum_scatter(
            part_v.astype(jnp.bfloat16), "seq", scatter_dimension=1, tiled=True
        ).astype(jnp.float32),
    )
    low_k = summed_k.astype(jnp.bfloat16)
    low_v = summed_v.astype(jnp.bfloat16)
    low_q = (grad_q * factor).astype(jnp.bfloat16)
    slope_query = outer_sum(normed_one, low_q)
    slope_query_bias = row_total(low_q)
    slope_key = outer_sum(normed_one, low_k)
    slope_value = outer_sum(normed_one, low_v)
    slope_value_bias = row_total(low_v)
    grad_normed = (
        linear_back(low_q, w_query) + linear_back(low_k, w_key) + linear_back(low_v, w_value)
    )
    grad_norm_one, slope_gain_one, slope_bias_one = norm_back_one(grad_normed)
    tokens_gradient = (grad_self + grad_norm_one).astype(jnp.bfloat16)
    owned = (
        lax.psum_scatter(slope_query, "grp", scatter_dimension=0, tiled=True),
        lax.psum_scatter(slope_key, "grp", scatter_dimension=0, tiled=True),
        lax.psum_scatter(slope_value, "grp", scatter_dimension=0, tiled=True),
        lax.psum_scatter(slope_mixer, "grp", scatter_dimension=0, tiled=True),
        lax.psum_scatter(slope_xquery, "grp", scatter_dimension=0, tiled=True),
        lax.psum_scatter(slope_xkey, "grp", scatter_dimension=0, tiled=True),
        lax.psum_scatter(slope_xvalue, "grp", scatter_dimension=0, tiled=True),
        lax.psum_scatter(slope_xmixer, "grp", scatter_dimension=0, tiled=True),
        lax.psum_scatter(slope_expand, "grp", scatter_dimension=0, tiled=True),
        lax.psum_scatter(slope_reduce, "grp", scatter_dimension=0, tiled=True),
        lax.psum_scatter(slope_gain_one, "grp", scatter_dimension=0, tiled=True),
        lax.psum_scatter(slope_bias_one, "grp", scatter_dimension=0, tiled=True),
        lax.psum_scatter(slope_query_bias, "grp", scatter_dimension=0, tiled=True),
        lax.psum_scatter(slope_value_bias, "grp", scatter_dimension=0, tiled=True),
        lax.psum_scatter(slope_mixer_bias, "grp", scatter_dimension=0, tiled=True),
        lax.psum_scatter(slope_gain_two, "grp", scatter_dimension=0, tiled=True),
        lax.psum_scatter(slope_bias_two, "grp", scatter_dimension=0, tiled=True),
        lax.psum_scatter(slope_xquery_bias, "grp", scatter_dimension=0, tiled=True),
        lax.psum_scatter(slope_xvalue_bias, "grp", scatter_dimension=0, tiled=True),
        lax.psum_scatter(slope_xmixer_bias, "grp", scatter_dimension=0, tiled=True),
        lax.psum_scatter(slope_gain_three, "grp", scatter_dimension=0, tiled=True),
        lax.psum_scatter(slope_bias_three, "grp", scatter_dimension=0, tiled=True),
        lax.psum_scatter(slope_expand_bias, "grp", scatter_dimension=0, tiled=True),
        lax.psum_scatter(slope_reduce_bias, "grp", scatter_dimension=0, tiled=True),
    )
    matrices = (
        lax.psum_scatter(
            owned[0].astype(jnp.bfloat16), "seq", scatter_dimension=1, tiled=True
        ).astype(jnp.float32),
        lax.psum_scatter(
            owned[1].astype(jnp.bfloat16), "seq", scatter_dimension=1, tiled=True
        ).astype(jnp.float32),
        lax.psum_scatter(
            owned[2].astype(jnp.bfloat16), "seq", scatter_dimension=1, tiled=True
        ).astype(jnp.float32),
        lax.psum_scatter(
            owned[3].astype(jnp.bfloat16), "seq", scatter_dimension=1, tiled=True
        ).astype(jnp.float32),
        lax.psum_scatter(
            owned[4].astype(jnp.bfloat16), "seq", scatter_dimension=1, tiled=True
        ).astype(jnp.float32),
        lax.psum_scatter(
            owned[5].astype(jnp.bfloat16), "seq", scatter_dimension=1, tiled=True
        ).astype(jnp.float32),
        lax.psum_scatter(
            owned[6].astype(jnp.bfloat16), "seq", scatter_dimension=1, tiled=True
        ).astype(jnp.float32),
        lax.psum_scatter(
            owned[7].astype(jnp.bfloat16), "seq", scatter_dimension=1, tiled=True
        ).astype(jnp.float32),
        lax.psum_scatter(
            owned[8].astype(jnp.bfloat16), "seq", scatter_dimension=1, tiled=True
        ).astype(jnp.float32),
        lax.psum_scatter(
            owned[9].astype(jnp.bfloat16), "seq", scatter_dimension=1, tiled=True
        ).astype(jnp.float32),
    )
    smaller = lax.psum(
        (
            owned[10],
            owned[11],
            owned[12],
            owned[13],
            owned[14],
            owned[15],
            owned[16],
            owned[17],
            owned[18],
            owned[19],
            owned[20],
            owned[21],
            owned[22],
            owned[23],
        ),
        "seq",
    )
    return (
        layer_output,
        tokens_gradient,
        smaller[0],
        smaller[1],
        matrices[0],
        smaller[2],
        matrices[1],
        matrices[2],
        smaller[3],
        matrices[3],
        smaller[4],
        smaller[5],
        smaller[6],
        matrices[4],
        smaller[7],
        matrices[5],
        matrices[6],
        smaller[8],
        matrices[7],
        smaller[9],
        smaller[10],
        smaller[11],
        matrices[8],
        smaller[12],
        matrices[9],
        smaller[13],
    )


def solution(mesh):
    placed = (
        P("grp", "seq", None),
        P("grp", "seq", None),
        P("grp"),
        P("grp"),
        P("grp"),
        P(),
        P("grp", "seq", None),
        P("grp"),
        P("grp"),
        P("grp", "seq"),
        P("grp"),
        P("grp", "seq"),
        P("grp", "seq"),
        P("grp"),
        P("grp", "seq"),
        P("grp"),
        P("grp"),
        P("grp"),
        P("grp", "seq"),
        P("grp"),
        P("grp", "seq"),
        P("grp", "seq"),
        P("grp"),
        P("grp", "seq"),
        P("grp"),
        P("grp"),
        P("grp"),
        P("grp", "seq"),
        P("grp"),
        P("grp", "seq"),
        P("grp"),
    )
    return jax.shard_map(
        on_device,
        mesh=mesh,
        in_specs=placed,
        out_specs=(
            P("grp", "seq", None),
            P("grp", "seq", None),
            P("grp"),
            P("grp"),
            P("grp", "seq"),
            P("grp"),
            P("grp", "seq"),
            P("grp", "seq"),
            P("grp"),
            P("grp", "seq"),
            P("grp"),
            P("grp"),
            P("grp"),
            P("grp", "seq"),
            P("grp"),
            P("grp", "seq"),
            P("grp", "seq"),
            P("grp"),
            P("grp", "seq"),
            P("grp"),
            P("grp"),
            P("grp"),
            P("grp", "seq"),
            P("grp"),
            P("grp", "seq"),
            P("grp"),
        ),
        check_vma=False,
    )
```

profile of v0, /device:TPU:1, one launch (start us, length us, event | category | flops | bytes accessed | tf_op | source)
XLA Modules:
  0.0 1710.4 jit_solution(6690577373234021959)
XLA Ops:
  7.4 26.5 %all_gather.120 = bf16[768,192]{1,0:T(8,128)(2,1)S(1)} all-gather(bf16[96,192]{1,0:T(8,128)(2,1)} %param.42), channel_id=1, replica_groups=mesh['grp'=8,'seq'=4] {'grp'}, dimensions={0}, use_global_device_ids=true | all-gather | bytes 331776 | tf_op jit(solution)/shard_map/all_gather | solution.py:131
  34.9 25.0 %all_gather.113 = bf16[768,192]{1,0:T(8,128)(2,1)S(1)} all-gather(bf16[96,192]{1,0:T(8,128)(2,1)} %param.43), channel_id=1, replica_groups=mesh['grp'=8,'seq'=4] {'grp'}, dimensions={0}, use_global_device_ids=true | all-gather | bytes 331776 | tf_op jit(solution)/shard_map/all_gather | solution.py:132
  61.6 25.1 %all_gather.117 = bf16[768,192]{1,0:T(8,128)(2,1)S(1)} all-gather(bf16[96,192]{1,0:T(8,128)(2,1)} %param.40), channel_id=1, replica_groups=mesh['grp'=8,'seq'=4] {'grp'}, dimensions={0}, use_global_device_ids=true | all-gather | bytes 331776 | tf_op jit(solution)/shard_map/all_gather | solution.py:130
  92.6 29.6 %all-reduce.29 = (bf16[768]{0:T(1024)(128)(2,1)S(1)}, bf16[768]{0:T(1024)(128)(2,1)S(1)}, bf16[768]{0:T(1024)(128)(2,1)S(1)}, bf16[768]{0:T(1024)(128)(2,1)S(1)}...) all-reduce(bf16[768]{0:T(1024)(128)(2,1)S(1)} %dynamic-update-slice, ...), channel_id=1, replica_groups=mesh['grp'=8,'seq'=4] {'grp'}, use_global_device_ids=true, to_apply=%add.8 | all-reduce | flops 9984 | bytes 39936
  128.6 25.4 %all_gather.123 = bf16[768,192]{1,0:T(8,128)(2,1)S(1)} all-gather(bf16[96,192]{1,0:T(8,128)(2,1)S(1)} %copy-done.43), channel_id=1, replica_groups=mesh['grp'=8,'seq'=4] {'grp'}, dimensions={0}, use_global_device_ids=true | all-gather | bytes 331776 | tf_op jit(solution)/shard_map/all_gather | solution.py:133
  155.1 25.2 %all_gather.132 = bf16[768,192]{1,0:T(8,128)(2,1)S(1)} all-gather(bf16[96,192]{1,0:T(8,128)(2,1)S(1)} %copy-done.44), channel_id=1, replica_groups=mesh['grp'=8,'seq'=4] {'grp'}, dimensions={0}, use_global_device_ids=true | all-gather | bytes 331776 | tf_op jit(solution)/shard_map/all_gather | solution.py:134
  181.2 25.2 %all_gather.127 = bf16[768,192]{1,0:T(8,128)(2,1)S(1)} all-gather(bf16[96,192]{1,0:T(8,128)(2,1)S(1)} %copy-done.45), channel_id=1, replica_groups=mesh['grp'=8,'seq'=4] {'grp'}, dimensions={0}, use_global_device_ids=true | all-gather | bytes 331776 | tf_op jit(solution)/shard_map/all_gather | solution.py:136
  208.1 25.0 %all_gather.135 = bf16[768,192]{1,0:T(8,128)(2,1)S(1)} all-gather(bf16[96,192]{1,0:T(8,128)(2,1)S(1)} %copy-done.46), channel_id=1, replica_groups=mesh['grp'=8,'seq'=4] {'grp'}, dimensions={0}, use_global_device_ids=true | all-gather | bytes 331776 | tf_op jit(solution)/shard_map/all_gather | solution.py:135
  234.0 24.8 %all_gather.137 = bf16[768,192]{1,0:T(8,128)(2,1)S(1)} all-gather(bf16[96,192]{1,0:T(8,128)(2,1)S(1)} %copy-done.47), channel_id=1, replica_groups=mesh['grp'=8,'seq'=4] {'grp'}, dimensions={0}, use_global_device_ids=true | all-gather | bytes 331776 | tf_op jit(solution)/shard_map/all_gather | solution.py:137
  303.7 32.4 %all-gather.29.cloned.1.call-done = bf16[2,1500,768]{2,0,1:T(2,128)(2,1)} async-done(((bf16[2,375,768]{2,0,1:T(2,128)(2,1)}), bf16[2,1500,768]{2,0,1:T(2,128)(2,1)}) %all-gather.29.cloned.1.call-update) | async-done | bytes 4608016 | tf_op jit(solution)/shard_map/all_gather | solution.py:196
  389.3 23.7 %all-gather.41.cloned.1.call-done = bf16[768,3072]{1,0:T(8,128)(2,1)} async-done(((bf16[768,768]{1,0:T(8,128)(2,1)}), bf16[768,3072]{1,0:T(8,128)(2,1)}) %all-gather.41.cloned.1.call-update) | async-done | bytes 4718608 | tf_op jit(solution)/shard_map/all_gather | solution.py:164
  418.3 33.7 %all-gather.45.cloned.1.call-done = bf16[3072,768]{0,1:T(8,128)(2,1)} async-done(((bf16[3072,192]{0,1:T(8,128)(2,1)}), bf16[3072,768]{0,1:T(8,128)(2,1)}) %all-gather.45.cloned.1.call-update) | async-done | bytes 4718608 | tf_op jit(solution)/shard_map/all_gather | solution.py:165
  597.3 44.1 %reduce-scatter.59.cloned.1.call-done = f32[96,768]{1,0:T(8,128)} async-done(((f32[768,768]{1,0:T(8,128)}), f32[96,768]{1,0:T(8,128)}) %reduce-scatter.59.cloned.1.call-update) | async-done | bytes 294928 | tf_op jit(solution)/shard_map/reduce_scatter | solution.py:277
  643.2 69.7 %reduce-scatter.53.cloned.1.call-done = f32[96,768]{1,0:T(8,128)} async-done(((f32[768,768]{1,0:T(8,128)}), f32[96,768]{1,0:T(8,128)}) %reduce-scatter.53.cloned.1.call-update) | async-done | bytes 294928 | tf_op jit(solution)/shard_map/reduce_scatter | solution.py:274
  714.8 69.5 %reduce-scatter.51.cloned.1.call-done = f32[96,768]{1,0:T(8,128)} async-done(((f32[768,768]{1,0:T(8,128)}), f32[96,768]{1,0:T(8,128)}) %reduce-scatter.51.cloned.1.call-update) | async-done | bytes 294928 | tf_op jit(solution)/shard_map/reduce_scatter | solution.py:273
  786.1 69.7 %reduce-scatter.45.cloned.1.call-done = f32[96,768]{1,0:T(8,128)} async-done(((f32[768,768]{1,0:T(8,128)}), f32[96,768]{1,0:T(8,128)}) %reduce-scatter.45.cloned.1.call-update) | async-done | bytes 294928 | tf_op jit(solution)/shard_map/reduce_scatter | solution.py:270
  857.7 69.7 %reduce-scatter.79.cloned.1.call-done = f32[96,768]{1,0:T(8,128)} async-done(((f32[768,768]{1,0:T(8,128)}), f32[96,768]{1,0:T(8,128)}) %reduce-scatter.79.cloned.1.call-update) | async-done | bytes 294928
  929.3 69.9 %reduce-scatter.77.cloned.1.call-done = f32[96,768]{1,0:T(8,128)} async-done(((f32[768,768]{1,0:T(8,128)}), f32[96,768]{1,0:T(8,128)}) %reduce-scatter.77.cloned.1.call-update) | async-done | bytes 294928
  1001.0 69.5 %reduce-scatter.49.cloned.1.call-done = f32[96,768]{1,0:T(8,128)} async-done(((f32[768,768]{1,0:T(8,128)}), f32[96,768]{1,0:T(8,128)}) %reduce-scatter.49.cloned.1.call-update) | async-done | bytes 294928 | tf_op jit(solution)/shard_map/reduce_scatter | solution.py:272
  1072.4 69.7 %reduce-scatter.47.cloned.1.call-done = f32[96,768]{1,0:T(8,128)} async-done(((f32[768,768]{1,0:T(8,128)}), f32[96,768]{1,0:T(8,128)}) %reduce-scatter.47.cloned.1.call-update) | async-done | bytes 294928 | tf_op jit(solution)/shard_map/reduce_scatter | solution.py:271
  1145.5 163.6 %reduce-scatter.65.cloned.1.call-done = f32[384,768]{1,0:T(8,128)} async-done(((f32[3072,768]{1,0:T(8,128)}), f32[384,768]{1,0:T(8,128)}) %reduce-scatter.65.cloned.1.call-update) | async-done | bytes 1179664 | tf_op jit(solution)/shard_map/reduce_scatter | solution.py:279
  1319.9 155.3 %reduce-scatter.61.cloned.1.call-done = f32[96,3072]{1,0:T(8,128)} async-done(((f32[768,3072]{1,0:T(8,128)}), f32[96,3072]{1,0:T(8,128)}) %reduce-scatter.61.cloned.1.call-update) | async-done | bytes 1179664 | tf_op jit(solution)/shard_map/reduce_scatter | solution.py:278
  1479.7 28.7 %all-reduce.27 = (f32[768]{0:T(1024)S(1)}, f32[768]{0:T(1024)S(1)}, f32[768]{0:T(1024)S(1)}, f32[768]{0:T(1024)S(1)}, f32[768]{0:T(1024)S(1)}, /*index=5*/f32[76...) all-reduce(f32[768]{0:T(1024)S(1)} %get-tuple-element.134, ...), channel_id=4, replica_groups=mesh['grp'=8,'seq'=4] {'grp'}, use_global_device_ids=true, to_apply=%region_22.23.clone | all-reduce | flops 13056 | bytes 104448
  1654.2 23.0 %reduce-scatter.83.cloned.1.call-done = bf16[192,384]{1,0:T(8,128)(2,1)} async-done(((bf16[768,384]{1,0:T(8,128)(2,1)}), bf16[192,384]{1,0:T(8,128)(2,1)}) %reduce-scatter.83.cloned.1.call-update) | async-done | bytes 147472
  (490 shorter events, 467.8 us)
Async XLA Ops:
  60.8 199.0 %all-gather.39.cloned.1.call-start = ((), (), s32[]{:S(2)}) async-start(), calls=%async_computation.33 | async-start | bytes 1327104 | tf_op jit(solution)/shard_map/all_gather | solution.py:138
  61.6 221.2 %all-gather.21.cloned.1.call-start = ((), (), s32[]{:S(2)}) async-start(), calls=%async_computation.24 | async-start | bytes 1474560 | tf_op jit(solution)/shard_map/all_gather | solution.py:156
  87.6 197.3 %all-gather.43.cloned.1.call-start = ((), (), s32[]{:S(2)}) async-start(), calls=%async_computation.35 | async-start | bytes 1327104 | tf_op jit(solution)/shard_map/all_gather | solution.py:139
  88.2 197.1 %all-gather.25.cloned.1.call-start = ((), (), s32[]{:S(2)}) async-start(), calls=%async_computation.26 | async-start | bytes 1720320 | tf_op jit(solution)/shard_map/all_gather | solution.py:188
  260.3 191.6 %all-gather.45.cloned.1.call-start = ((), (), s32[]{:S(2)}) async-start(), calls=%async_computation.36 | async-start | bytes 5898240 | tf_op jit(solution)/shard_map/all_gather | solution.py:165
  285.0 291.5 %reduce-scatter.43.cloned.1.call-start = ((), (), s32[]{:S(2)}) async-start(), calls=%async_computation.38 | async-start | bytes 1720320 | tf_op jit(solution)/shard_map/reduce_scatter | solution.py:252
  533.8 250.4 %reduce-scatter.51.cloned.1.call-start = ((), (), s32[]{:S(2)}) async-start(), calls=%async_computation.42 | async-start | bytes 2654208 | tf_op jit(solution)/shard_map/reduce_scatter | solution.py:273
  535.9 320.0 %reduce-scatter.45.cloned.1.call-start = ((), (), s32[]{:S(2)}) async-start(), calls=%async_computation.39 | async-start | bytes 2654208 | tf_op jit(solution)/shard_map/reduce_scatter | solution.py:270
  541.5 385.9 %reduce-scatter.79.cloned.1.call-start = ((), (), s32[]{:S(2)}) async-start(), calls=%async_computation.56 | async-start | bytes 2654208
  560.6 438.6 %reduce-scatter.77.cloned.1.call-start = ((), (), s32[]{:S(2)}) async-start(), calls=%async_computation.55 | async-start | bytes 2654208
  576.4 494.2 %reduce-scatter.49.cloned.1.call-start = ((), (), s32[]{:S(2)}) async-start(), calls=%async_computation.41 | async-start | bytes 2654208 | tf_op jit(solution)/shard_map/reduce_scatter | solution.py:272
  579.6 562.6 %reduce-scatter.47.cloned.1.call-start = ((), (), s32[]{:S(2)}) async-start(), calls=%async_computation.40 | async-start | bytes 2654208 | tf_op jit(solution)/shard_map/reduce_scatter | solution.py:271
  582.7 726.4 %reduce-scatter.65.cloned.1.call-start = ((), (), s32[]{:S(2)}) async-start(), calls=%async_computation.49 | async-start | bytes 10616832 | tf_op jit(solution)/shard_map/reduce_scatter | solution.py:279
  589.9 885.2 %reduce-scatter.61.cloned.1.call-start = ((), (), s32[]{:S(2)}) async-start(), calls=%async_computation.47 | async-start | bytes 10616832 | tf_op jit(solution)/shard_map/reduce_scatter | solution.py:278
  597.2 926.8 %reduce-scatter.81.cloned.1.call-start = ((), (), s32[]{:S(2)}) async-start(), calls=%async_computation.57 | async-start | bytes 245760
  643.1 882.4 %reduce-scatter.75.cloned.1.call-start = ((), (), s32[]{:S(2)}) async-start(), calls=%async_computation.54 | async-start | bytes 245760
  714.7 826.0 %reduce-scatter.73.cloned.1.call-start = ((), (), s32[]{:S(2)}) async-start(), calls=%async_computation.53 | async-start | bytes 245760
  786.1 777.4 %reduce-scatter.67.cloned.1.call-start = ((), (), s32[]{:S(2)}) async-start(), calls=%async_computation.50 | async-start | bytes 245760
  857.7 728.0 %reduce-scatter.57.cloned.1.call-start = ((), (), s32[]{:S(2)}) async-start(), calls=%async_computation.45 | async-start | bytes 245760 | tf_op jit(solution)/shard_map/reduce_scatter | solution.py:314
  929.3 678.5 %reduce-scatter.55.cloned.1.call-start = ((), (), s32[]{:S(2)}) async-start(), calls=%async_computation.44 | async-start | bytes 245760 | tf_op jit(solution)/shard_map/reduce_scatter | solution.py:311
  1001.0 628.9 %reduce-scatter.71.cloned.1.call-start = ((), (), s32[]{:S(2)}) async-start(), calls=%async_computation.52 | async-start | bytes 245760
  1072.4 580.3 %reduce-scatter.69.cloned.1.call-start = ((), (), s32[]{:S(2)}) async-start(), calls=%async_computation.51 | async-start | bytes 245760
  1143.9 533.3 %reduce-scatter.83.cloned.1.call-start = ((), (), s32[]{:S(2)}) async-start(), calls=%async_computation.58 | async-start | bytes 737280
  1311.6 390.2 %reduce-scatter.63.cloned.1.call-start = ((), (), s32[]{:S(2)}) async-start(), calls=%async_computation.48 | async-start | bytes 737280 | tf_op jit(solution)/shard_map/reduce_scatter | solution.py:320
  (114 other events, 8068.2 us)
Sparse Core Ops, SparseCore 0:
  35.0 24.8 all-gather.22
  62.0 30.0 all-gather.16
  94.2 39.9 all-gather.38
  155.8 42.8 all-gather.42
  299.3 36.8 all-gather.28
  375.5 37.4 all-gather.40
  414.5 37.4 all-gather.44
  513.9 26.5 reduce-scatter.42
  543.0 26.9 reduce-scatter.40
  573.3 67.9 reduce-scatter.58
  644.8 68.0 reduce-scatter.52
  716.3 67.9 reduce-scatter.50
  787.8 68.0 reduce-scatter.44
  859.3 68.0 reduce-scatter.78
  930.9 68.1 reduce-scatter.76
  1002.5 67.9 reduce-scatter.48
  1074.1 68.0 reduce-scatter.46
  1145.6 163.5 reduce-scatter.64
  1312.6 162.5 reduce-scatter.60
  1498.8 19.7 reduce-scatter.74
  1520.8 19.8 reduce-scatter.72
  1565.9 19.7 reduce-scatter.56
  1655.0 22.1 reduce-scatter.82
  1679.6 22.0 reduce-scatter.62
  (13 shorter events, 238.9 us)
where the time goes:
time: 1720 us; the launch traced here: 1710 us
  waiting for transfers between devices  1110 us (65%)
  blocking collectives  296 us (17%)
  matrix products  170 us (10%)
  local copies, waits for them, and re-layouts  71.7 us (4%)
  other arithmetic  41.8 us (2%)
  between operations  18.5 us (1%)
    unnamed x46, waiting for transfers between devices  242 us
    reduce_scatter x1, waiting for transfers between devices, on_device(): lax.psum_scatter(slope_reduce, 'grp', scatter_dimension=0, tiled=True)  164 us
    reduce_scatter x1, waiting for transfers between devices, on_device(): lax.psum_scatter(slope_expand, 'grp', scatter_dimension=0, tiled=True)  155 us
    reduce_scatter x1, waiting for transfers between devices, on_device(): lax.psum_scatter(slope_xquery, 'grp', scatter_dimension=0, tiled=True)  69.7 us
    reduce_scatter x1, waiting for transfers between devices, on_device(): lax.psum_scatter(slope_query, 'grp', scatter_dimension=0, tiled=True)  69.7 us
    reduce_scatter x1, waiting for transfers between devices, on_device(): lax.psum_scatter(slope_key, 'grp', scatter_dimension=0, tiled=True)  69.7 us
    reduce_scatter x1, waiting for transfers between devices, on_device(): lax.psum_scatter(slope_value, 'grp', scatter_dimension=0, tiled=True)  69.5 us
    reduce_scatter x1, waiting for transfers between devices, on_device(): lax.psum_scatter(slope_mixer, 'grp', scatter_dimension=0, tiled=True)  69.5 us
  transfers between devices with their start and end apart: 37, of which 22 were waited for; matrix products, arithmetic and copies ran while one was open for 12% of the time, Pallas kernels for 0%

commit v1 on v0

--- a/solution.py
+++ b/solution.py
@@ -3,6 +3,8 @@
 import jax
 import jax.numpy as jnp
 from jax import lax
+from jax.experimental import pallas as pl
+from jax.experimental.pallas import tpu as pltpu
 from jax.sharding import PartitionSpec as P
 
 HEADS = 12
@@ -93,7 +95,7 @@
     )
 
 
-def on_device(
+def on_device_plain(
     tokens,
     encoder_states,
     lengths,
@@ -373,6 +375,617 @@
     )
 
 
+MESH_ID = pl.DeviceIdType.MESH
+NZ, NX, NY, NC = 4, 2, 2, 2
+GROUPS = 8
+
+
+def where_am_i():
+    grp = lax.axis_index("grp")
+    seq = lax.axis_index("seq")
+    return grp // NX, lax.rem(grp, NX), seq // NC, lax.rem(seq, NC)
+
+
+def device_at(z, x, y, c):
+    return (z * NX + x, y * NC + c)
+
+
+def lanes(start, size):
+    return pl.ds(pl.multiple_of(start, 128), size)
+
+
+def pieces_of(bank, group, y, c, x, z_from, z_to):
+    pairs, wide, tall = bank
+    if group < 4:
+        return [pairs.at[group, y, pl.ds(z_from, z_to - z_from), x, :, lanes(c * 384, 384)]]
+    if group < 6:
+        start = (y * NC + c) * 768 + (group - 4) * 384
+        return [wide.at[pl.ds(z_from, z_to - z_from), x, :, lanes(start, 384)]]
+    return [
+        tall.at[y, c, pl.ds((group - 6) * 96, 96), lanes((z * NX + x) * 384, 384)]
+        for z in range(z_from, z_to)
+    ]
+
+
+def piece_at(bank, group, y, c, x, z):
+    pairs, wide, tall = bank
+    if group < 4:
+        return pairs.at[group, y, z, x, :, lanes(c * 384, 384)]
+    if group < 6:
+        return wide.at[z, x, :, lanes((y * NC + c) * 768 + (group - 4) * 384, 384)]
+    return tall.at[y, c, pl.ds((group - 6) * 96, 96), lanes((z * NX + x) * 384, 384)]
+
+
+def own_piece(bank, group):
+    pairs, wide, tall = bank
+    if group < 4:
+        return pairs.at[group]
+    if group < 6:
+        return wide.at[:, pl.ds((group - 4) * 384, 384)]
+    return tall.at[pl.ds((group - 6) * 96, 96), :]
+
+
+class Mail:
+    def __init__(self, send_sems, recv_sems):
+        self.send_sems, self.recv_sems, self.count, self.sent = send_sems, recv_sems, 0, []
+
+    def slots(self, number):
+        first = self.count
+        self.count += number
+        return list(range(first, first + number))
+
+    def post(self, source, target, slot, device):
+        copy = pltpu.make_async_remote_copy(
+            src_ref=source,
+            dst_ref=target,
+            send_sem=self.send_sems.at[slot],
+            recv_sem=self.recv_sems.at[slot],
+            device_id=device,
+            device_id_type=MESH_ID,
+        )
+        copy.start()
+        self.sent.append(copy)
+
+    def arrive(self, target, slot, device):
+        pltpu.make_async_remote_copy(
+            src_ref=target,
+            dst_ref=target,
+            send_sem=self.send_sems.at[slot],
+            recv_sem=self.recv_sems.at[slot],
+            device_id=device,
+            device_id_type=MESH_ID,
+        ).wait_recv()
+
+    def finish(self):
+        for copy in self.sent:
+            copy.wait_send()
+
+
+def greet(z, x, y, c):
+    barrier = pltpu.get_barrier_semaphore()
+    friends = [device_at(lax.rem(z + k, NZ), x, y, c) for k in range(1, NZ)]
+    friends += [device_at(lax.rem(z + k, NZ), 1 - x, y, c) for k in range(NZ)]
+    friends += [device_at(z, x, 1 - y, c), device_at(z, x, y, 1 - c)]
+    for friend in friends:
+        pl.semaphore_signal(barrier, inc=1, device_id=friend, device_id_type=MESH_ID)
+    pl.semaphore_wait(barrier, len(friends))
+
+
+def parts_in(group, number):
+    return number if group >= 6 else 1
+
+
+def gather_kernel(
+    pairs_in, wide_in, tall_in, small_in, frames_in, tokens_in,
+    pairs, wide, tall, small, frames, tokens,
+    send_sems, recv_sems, local_sems,
+):
+    z, x, y, c = where_am_i()
+    greet(z, x, y, c)
+    mail = Mail(send_sems, recv_sems)
+    own = (pairs_in, wide_in, tall_in)
+    bank = (pairs, wide, tall)
+    x_mate, y_mate = device_at(z, 1 - x, y, c), device_at(z, x, 1 - y, c)
+    c_mate = device_at(z, x, y, 1 - c)
+    z_mates = [device_at(lax.rem(z + k, NZ), x, y, c) for k in range(1, NZ)]
+    grp = z * NX + x
+    seq = y * NC + c
+
+    local = []
+
+    def keep(source, target):
+        copy = pltpu.make_async_copy(source, target, local_sems.at[len(local)])
+        copy.start()
+        local.append(copy)
+
+    small_slots = mail.slots(2 * NZ - 1)
+    small_to = z_mates + [device_at(lax.rem(z + k, NZ), 1 - x, y, c) for k in range(NZ)]
+    for slot, device in zip(small_slots, small_to):
+        mail.post(small_in, small.at[grp], slot, device)
+    keep(small_in, small.at[grp])
+    for group in range(GROUPS):
+        keep(own_piece(own, group), piece_at(bank, group, y, c, x, z))
+    keep(frames_in, frames.at[seq])
+    keep(tokens_in, tokens.at[seq])
+
+    z_slots = [mail.slots(NZ - 1) for _ in range(GROUPS)]
+
+    def to_column(group):
+        for k in range(1, NZ):
+            mail.post(
+                own_piece(own, group), piece_at(bank, group, y, c, x, z), z_slots[group][k - 1], z_mates[k - 1]
+            )
+
+    def post_all(group, slots, device, yy, cc, xx, z_from, z_to):
+        for slot, ref in zip(slots, pieces_of(bank, group, yy, cc, xx, z_from, z_to)):
+            mail.post(ref, ref, slot, device)
+
+    def arrive_all(group, slots, device, yy, cc, xx, z_from, z_to):
+        for slot, ref in zip(slots, pieces_of(bank, group, yy, cc, xx, z_from, z_to)):
+            mail.arrive(ref, slot, device)
+
+    x_slots = [mail.slots(parts_in(g, 4)) for g in range(GROUPS)]
+    y_slots = [mail.slots(parts_in(g, 4)) for g in range(GROUPS)]
+    dy_slots = [mail.slots(parts_in(g, 2)) for g in range(GROUPS)]
+    dx_slots = [mail.slots(parts_in(g, 2)) for g in range(GROUPS)]
+    co_slots = [mail.slots(parts_in(g, 4)) for g in range(GROUPS)]
+    cx_slots = [mail.slots(parts_in(g, 4)) for g in range(GROUPS)]
+    cy_slots = [mail.slots(parts_in(g, 4)) for g in range(GROUPS)]
+    cd_slots = [mail.slots(2 * parts_in(g, 2)) for g in range(GROUPS)]
+    token_slots = mail.slots(3)
+    frame_slots = mail.slots(3)
+
+    def spread(group):
+        for k in range(1, NZ):
+            zz = lax.rem(z + NZ - k, NZ)
+            mail.arrive(piece_at(bank, group, y, c, x, zz), z_slots[group][k - 1], z_mates[k - 1])
+        local[1 + group].wait()
+        post_all(group, x_slots[group], x_mate, y, c, x, 0, 4)
+        post_all(group, y_slots[group], y_mate, y, c, x, 0, 4)
+        post_all(group, co_slots[group], c_mate, y, c, x, 0, 4)
+
+    def turn(group):
+        arrive_all(group, x_slots[group], x_mate, y, c, 1 - x, 0, 4)
+        post_all(group, dy_slots[group], y_mate, y, c, 1 - x, 0, 2)
+        post_all(group, cx_slots[group], c_mate, y, c, 1 - x, 0, 4)
+        arrive_all(group, y_slots[group], y_mate, 1 - y, c, x, 0, 4)
+        post_all(group, dx_slots[group], x_mate, 1 - y, c, x, 2, 4)
+        post_all(group, cy_slots[group], c_mate, 1 - y, c, x, 0, 4)
+
+    def share(group):
+        half = parts_in(group, 2)
+        arrive_all(group, dy_slots[group], y_mate, 1 - y, c, 1 - x, 0, 2)
+        post_all(group, cd_slots[group][:half], c_mate, 1 - y, c, 1 - x, 0, 2)
+        arrive_all(group, dx_slots[group], x_mate, 1 - y, c, 1 - x, 2, 4)
+        post_all(group, cd_slots[group][half:], c_mate, 1 - y, c, 1 - x, 2, 4)
+
+    def complete(group):
+        half = parts_in(group, 2)
+        arrive_all(group, co_slots[group], c_mate, y, 1 - c, x, 0, 4)
+        arrive_all(group, cx_slots[group], c_mate, y, 1 - c, 1 - x, 0, 4)
+        arrive_all(group, cy_slots[group], c_mate, 1 - y, 1 - c, x, 0, 4)
+        arrive_all(group, cd_slots[group][:half], c_mate, 1 - y, 1 - c, 1 - x, 0, 2)
+        arrive_all(group, cd_slots[group][half:], c_mate, 1 - y, 1 - c, 1 - x, 2, 4)
+
+    def swap_rows(source, bank_rows, slots, first):
+        if first:
+            mail.post(source, bank_rows.at[seq], slots[0], y_mate)
+            mail.post(source, bank_rows.at[seq], slots[1], c_mate)
+        else:
+            other = (1 - y) * NC + c
+            mail.arrive(bank_rows.at[other], slots[0], y_mate)
+            mail.post(bank_rows.at[other], bank_rows.at[other], slots[2], c_mate)
+
+    def rows_done(bank_rows, slots):
+        mail.arrive(bank_rows.at[y * NC + 1 - c], slots[1], c_mate)
+        mail.arrive(bank_rows.at[(1 - y) * NC + 1 - c], slots[2], c_mate)
+
+    to_column(0)
+    to_column(1)
+    swap_rows(tokens_in, tokens, token_slots, True)
+    swap_rows(frames_in, frames, frame_slots, True)
+    for step in range(GROUPS + 3):
+        if step + 2 < GROUPS:
+            to_column(step + 2)
+        if step < GROUPS:
+            spread(step)
+        if 0 <= step - 1 < GROUPS:
+            turn(step - 1)
+        if 0 <= step - 2 < GROUPS:
+            share(step - 2)
+        if 0 <= step - 3 < GROUPS:
+            complete(step - 3)
+        if step == 1:
+            swap_rows(tokens_in, tokens, token_slots, False)
+        if step == 3:
+            swap_rows(frames_in, frames, frame_slots, False)
+    rows_done(tokens, token_slots)
+    rows_done(frames, frame_slots)
+    for k in range(1, NZ):
+        zz = lax.rem(z + NZ - k, NZ)
+        mail.arrive(small.at[zz * NX + x], small_slots[k - 1], z_mates[k - 1])
+    for k in range(NZ):
+        zz = lax.rem(z + NZ - k, NZ)
+        mail.arrive(small.at[zz * NX + 1 - x], small_slots[NZ - 1 + k], x_mate)
+    for number, copy in enumerate(local):
+        if not 1 <= number <= GROUPS:
+            copy.wait()
+    mail.finish()
+
+
+def slots_needed():
+    return (2 * NZ - 1) + 6 + sum(3 + parts_in(g, 4) * 5 + parts_in(g, 2) * 4 for g in range(GROUPS))
+
+
+def gather_everything(pairs, wide, tall, small, frames, tokens):
+    bf16 = jnp.bfloat16
+    number = slots_needed()
+    anywhere = pl.BlockSpec(memory_space=pl.ANY)
+    return pl.pallas_call(
+        gather_kernel,
+        out_shape=(
+            jax.ShapeDtypeStruct((4, NY, NZ, NX, 96, 768), bf16),
+            jax.ShapeDtypeStruct((NZ, NX, 96, 3072), bf16),
+            jax.ShapeDtypeStruct((NY, NC, 192, 3072), bf16),
+            jax.ShapeDtypeStruct((NZ * NX,) + small.shape, bf16),
+            jax.ShapeDtypeStruct((NY * NC,) + frames.shape, bf16),
+            jax.ShapeDtypeStruct((NY * NC,) + tokens.shape, bf16),
+        ),
+        in_specs=[anywhere] * 6,
+        out_specs=(anywhere,) * 6,
+        scratch_shapes=[
+            pltpu.SemaphoreType.DMA((number,)),
+            pltpu.SemaphoreType.DMA((number,)),
+            pltpu.SemaphoreType.DMA((GROUPS + 3,)),
+        ],
+        compiler_params=pltpu.CompilerParams(collective_id=1, has_side_effects=True),
+        name="gather_all",
+    )(pairs, wide, tall, small, frames, tokens)
+
+
+def reduce_kernel(
+    pairs, wide, tall, small,
+    total, small_total,
+    own_acc, core_in, diag_in, x_in, y_in, z_in, small_in, small_sum, small_seq,
+    send_sems, recv_sems, local_sems,
+):
+    z, x, y, c = where_am_i()
+    greet(z, x, y, c)
+    mail = Mail(send_sems, recv_sems)
+    bank = (pairs, wide, tall)
+    x_mate, y_mate = device_at(z, 1 - x, y, c), device_at(z, x, 1 - y, c)
+    c_mate = device_at(z, x, y, 1 - c)
+    z_mates = [device_at(lax.rem(z + k, NZ), x, y, c) for k in range(1, NZ)]
+    grp = z * NX + x
+    seq = y * NC + c
+
+    small_slots = mail.slots(2 * NZ - 1)
+    small_to = [(lax.rem(z + k, NZ), x) for k in range(1, NZ)]
+    small_to += [(lax.rem(z + k, NZ), 1 - x) for k in range(NZ)]
+    for number, (zz, xx) in enumerate(small_to):
+        mail.post(small.at[zz * NX + xx], small_in.at[number], small_slots[number], device_at(zz, xx, y, c))
+
+    core_slots = [mail.slots(4 * parts_in(g, 4)) for g in range(GROUPS)]
+    local = []
+    count = 0
+    columns = [(0, 0), (1, 0), (0, 1), (1, 1)]
+
+    def column(dx, dy):
+        return jnp.where(dx, 1 - x, x), jnp.where(dy, 1 - y, y)
+
+    for group in range(GROUPS):
+        mine = []
+        for place, (dx, dy) in enumerate(columns):
+            xx, yy = (1 - x if dx else x), (1 - y if dy else y)
+            targets = [core_in.at[group, place]] if group < 6 else [core_in.at[group, place, k] for k in range(4)]
+            sources = pieces_of(bank, group, yy, 1 - c, xx, 0, 4)
+            many = len(sources)
+            for k in range(many):
+                mail.post(sources[k], targets[k], core_slots[group][place * many + k], c_mate)
+            sources = pieces_of(bank, group, yy, c, xx, 0, 4)
+            targets = [own_acc.at[group, place]] if group < 6 else [own_acc.at[group, place, k] for k in range(4)]
+            for k in range(many):
+                copy = pltpu.make_async_copy(sources[k], targets[k], local_sems.at[count])
+                copy.start()
+                mine.append(copy)
+                count += 1
+        local.append(mine)
+
+    dx_slots = [mail.slots(1) for _ in range(GROUPS)]
+    dy_slots = [mail.slots(1) for _ in range(GROUPS)]
+    x_slots = [mail.slots(1) for _ in range(GROUPS)]
+    y_slots = [mail.slots(1) for _ in range(GROUPS)]
+    z_slots = [mail.slots(NZ - 1) for _ in range(GROUPS)]
+
+    def core_step(group):
+        for copy in local[group]:
+            copy.wait()
+        many = 4 if group >= 6 else 1
+        for place in (3, 1, 2, 0):
+            for k in range(many):
+                target = core_in.at[group, place] if many == 1 else core_in.at[group, place, k]
+                mail.arrive(target, core_slots[group][place * many + k], c_mate)
+
+            def add(k, carry):
+                own_acc[group, place, k] = own_acc[group, place, k] + core_in[group, place, k]
+                return carry
+
+            lax.fori_loop(0, 4, add, 0)
+            if place == 3:
+                mail.post(own_acc.at[group, 3, pl.ds(0, 2)], diag_in.at[group, 0], dx_slots[group][0], x_mate)
+                mail.post(own_acc.at[group, 3, pl.ds(2, 2)], diag_in.at[group, 1], dy_slots[group][0], y_mate)
+
+    def side_step(group):
+        mail.arrive(diag_in.at[group, 0], dx_slots[group][0], x_mate)
+
+        def add_y(k, carry):
+            own_acc[group, 2, k] = own_acc[group, 2, k] + diag_in[group, 0, k]
+            return carry
+
+        lax.fori_loop(0, 2, add_y, 0)
+        mail.post(own_acc.at[group, 2], y_in.at[group], y_slots[group][0], y_mate)
+        mail.arrive(diag_in.at[group, 1], dy_slots[group][0], y_mate)
+
+        def add_x(k, carry):
+            own_acc[group, 1, k + 2] = own_acc[group, 1, k + 2] + diag_in[group, 1, k]
+            return carry
+
+        lax.fori_loop(0, 2, add_x, 0)
+        mail.post(own_acc.at[group, 1], x_in.at[group], x_slots[group][0], x_mate)
+
+    def column_step(group):
+        mail.arrive(y_in.at[group], y_slots[group][0], y_mate)
+        mail.arrive(x_in.at[group], x_slots[group][0], x_mate)
+
+        def add(k, carry):
+            own_acc[group, 0, k] = (
+                own_acc[group, 0, k].astype(jnp.float32)
+                + x_in[group, k].astype(jnp.float32)
+                + y_in[group, k].astype(jnp.float32)
+            ).astype(jnp.bfloat16)
+            return carry
+
+        lax.fori_loop(0, 4, add, 0)
+        for k in range(1, NZ):
+            zz = lax.rem(z + k, NZ)
+            mail.post(own_acc.at[group, 0, zz], z_in.at[group, k - 1], z_slots[group][k - 1], z_mates[k - 1])
+
+    def last_step(group):
+        for k in range(1, NZ):
+            mail.arrive(z_in.at[group, k - 1], z_slots[group][k - 1], z_mates[k - 1])
+        total[group] = own_acc[group, 0, z].astype(jnp.float32) + (
+            z_in[group, 0].astype(jnp.float32) + z_in[group, 1].astype(jnp.float32)
+        ) + z_in[group, 2].astype(jnp.float32)
+
+    seq_slots = mail.slots(3)
+    for step in range(GROUPS + 3):
+        if step < GROUPS:
+            core_step(step)
+        if 0 <= step - 1 < GROUPS:
+            side_step(step - 1)
+        if 0 <= step - 2 < GROUPS:
+            column_step(step - 2)
+        if 0 <= step - 3 < GROUPS:
+            last_step(step - 3)
+        if step == 3:
+            for number in range(2 * NZ - 1):
+                mail.arrive(small_in.at[number], small_slots[number], x_mate)
+            small_sum[...] = (
+                (small[grp] + small_in[0]) + (small_in[1] + small_in[2])
+                + ((small_in[3] + small_in[4]) + (small_in[5] + small_in[6]))
+            )
+            mail.post(small_sum, small_seq.at[0], seq_slots[0], c_mate)
+        if step == 5:
+            mail.arrive(small_seq.at[0], seq_slots[0], c_mate)
+            small_seq[1] = small_sum[...] + small_seq[0]
+            mail.post(small_seq.at[1], small_seq.at[2], seq_slots[1], y_mate)
+        if step == 7:
+            mail.arrive(small_seq.at[2], seq_slots[1], y_mate)
+            small_total[...] = small_seq[1] + small_seq[2]
+    mail.finish()
+
+
+def reduce_everything(pairs, wide, tall, small):
+    bf16 = jnp.bfloat16
+    piece = (96, 384)
+    number = 7 + 3 + sum(4 * parts_in(g, 4) + 4 + 3 for g in range(GROUPS))
+    anywhere = pl.BlockSpec(memory_space=pl.ANY)
+    inside = pl.BlockSpec(memory_space=pltpu.VMEM)
+    small_piece = small.shape[1:]
+    return pl.pallas_call(
+        reduce_kernel,
+        out_shape=(
+            jax.ShapeDtypeStruct((GROUPS,) + piece, jnp.float32),
+            jax.ShapeDtypeStruct(small_piece, jnp.float32),
+        ),
+        in_specs=[anywhere] * 3 + [inside],
+        out_specs=(inside, inside),
+        scratch_shapes=[
+            pltpu.VMEM((GROUPS, 4, NZ) + piece, bf16),
+            pltpu.VMEM((GROUPS, 4, NZ) + piece, bf16),
+            pltpu.VMEM((GROUPS, 2, 2) + piece, bf16),
+            pltpu.VMEM((GROUPS, NZ) + piece, bf16),
+            pltpu.VMEM((GROUPS, NZ) + piece, bf16),
+            pltpu.VMEM((GROUPS, NZ - 1) + piece, bf16),
+            pltpu.VMEM((7,) + small_piece, jnp.float32),
+            pltpu.VMEM(small_piece, jnp.float32),
+            pltpu.VMEM((3,) + small_piece, jnp.float32),
+            pltpu.SemaphoreType.DMA((number,)),
+            pltpu.SemaphoreType.DMA((number,)),
+            pltpu.SemaphoreType.DMA((4 * sum(parts_in(g, 4) for g in range(GROUPS)),)),
+        ],
+        compiler_params=pltpu.CompilerParams(
+            collective_id=2, has_side_effects=True, vmem_limit_bytes=58 << 20
+        ),
+        name="reduce_all",
+    )(pairs, wide, tall, small)
+
+
+def joined(first, second):
+    return jnp.concatenate([first, second], axis=1)
+
+
+def on_device_fast(*arguments):
+    (
+        tokens, encoder_states, lengths, frame_counts, corpus_ids, corpus_weights, cotangent,
+        first_gain, first_bias, query_weight, query_bias, key_weight, value_weight, value_bias,
+        output_weight, output_bias, second_gain, second_bias, cross_query_weight, cross_query_bias,
+        cross_key_weight, cross_value_weight, cross_value_bias, cross_output_weight, cross_output_bias,
+        third_gain, third_bias, expand_weight, expand_bias, reduce_weight, reduce_bias,
+    ) = arguments
+    bf16, f32 = jnp.bfloat16, jnp.float32
+    frame_span = encoder_states.shape[1]
+    small_vectors = (
+        first_gain, first_bias, query_bias, value_bias, output_bias, second_gain, second_bias,
+        cross_query_bias, cross_value_bias, cross_output_bias, third_gain, third_bias, expand_bias, reduce_bias,
+    )
+    sizes = [v.shape[0] for v in small_vectors]
+    small = jnp.pad(jnp.concatenate(small_vectors), (0, 2048 - sum(sizes))).reshape(16, 128)
+    pairs = jnp.stack([
+        joined(query_weight, key_weight),
+        joined(value_weight, cross_query_weight),
+        joined(cross_key_weight, cross_value_weight),
+        joined(output_weight, cross_output_weight),
+    ])
+    frames_padded = jnp.pad(encoder_states, ((0, 0), (0, 384 - frame_span), (0, 0)))
+    pairs_all, wide_all, tall_all, small_all, frames_got, tokens_got = gather_everything(
+        pairs, expand_weight, reduce_weight.T, small, frames_padded, tokens
+    )
+    pairs_all = pairs_all.reshape(4, NY, 768, NC, 2, 192)
+    plain = [
+        pairs_all[p, :, :, :, h].transpose(1, 0, 2, 3).reshape(768, 768) for p in range(4) for h in range(2)
+    ]
+    w_query, w_key, w_value, x_query, x_key, x_value, w_mixer, x_mixer = plain
+    w_expand = wide_all.reshape(768, 3072)
+    w_reduce = tall_all.reshape(768, 3072)
+    flat = small_all.reshape(8, 2048)
+    vectors, at = [], 0
+    for size in sizes:
+        vectors.append(flat[:, at:at + size].reshape(-1).astype(f32))
+        at += size
+    factor = 1.0 / math.sqrt(HEAD_DIM)
+    seq_count = lax.axis_size("seq")
+    span_rows = tokens.shape[1]
+    query_pos = lax.axis_index("seq") * span_rows + jnp.arange(span_rows, dtype=jnp.int32)
+    key_pos = jnp.arange(span_rows * seq_count, dtype=jnp.int32)
+    self_mask = (key_pos[None, None, :] <= query_pos[None, :, None]) & (
+        key_pos[None, None, :] < lengths[:, None, None]
+    )
+    frame_pos = jnp.arange(384 * seq_count, dtype=jnp.int32)
+    inside, block = frame_pos % 384, frame_pos // 384
+    cross_mask = (inside < frame_span)[None, None, :] & (
+        (block * frame_span + inside)[None, None, :] < frame_counts[:, None, None]
+    )
+    frames_all = frames_got.transpose(1, 0, 2, 3).reshape(2, 1536, 768)
+    tokens_all = tokens_got.transpose(1, 0, 2, 3).reshape(2, span_rows * seq_count, 768).astype(f32)
+    layer_in = tokens.astype(f32)
+    normed_all = norm_rows(tokens_all, vectors[0], vectors[1]).astype(bf16)
+    normed_one, norm_back_one = jax.vjp(norm_rows, layer_in, vectors[0], vectors[1])
+    normed_one = normed_one.astype(bf16)
+    query_low = ((linear(normed_one, w_query) + vectors[2]) * factor).astype(bf16)
+    key_all = linear(normed_all, w_key).astype(bf16)
+    value_all = (linear(normed_all, w_value) + vectors[3]).astype(bf16)
+    self_out, self_logsum = attend(query_low, key_all, value_all, self_mask)
+    after_self = layer_in + linear(self_out, w_mixer) + vectors[4]
+    normed_two, norm_back_two = jax.vjp(norm_rows, after_self, vectors[5], vectors[6])
+    normed_two = normed_two.astype(bf16)
+    cross_query = ((linear(normed_two, x_query) + vectors[7]) * factor).astype(bf16)
+    cross_keys_all = linear(frames_all, x_key).astype(bf16)
+    cross_values_all = (linear(frames_all, x_value) + vectors[8]).astype(bf16)
+    cross_out, cross_logsum = attend(cross_query, cross_keys_all, cross_values_all, cross_mask)
+    after_cross = after_self + linear(cross_out, x_mixer) + vectors[9]
+    normed_three, norm_back_three = jax.vjp(norm_rows, after_cross, vectors[10], vectors[11])
+    normed_three = normed_three.astype(bf16)
+    hidden = linear(normed_three, w_expand) + vectors[12]
+    gated, gate_back = jax.vjp(smooth_gate, hidden)
+    gated_low = gated.astype(bf16)
+    result = after_cross + linear_back(gated_low, w_reduce) + vectors[13]
+    layer_output = result.astype(bf16)
+    present = (query_pos[None, :] < lengths[:, None]).astype(f32)
+    corpus_index = jnp.arange(corpus_weights.shape[0], dtype=jnp.int32)
+    corpus_scale = jnp.sum(
+        jnp.where(corpus_ids[:, None] == corpus_index[None, :], corpus_weights[None, :], 0.0), axis=1
+    )
+    grad_out = cotangent.astype(f32) * (present * corpus_scale[:, None])[:, :, None]
+    reduce_low = grad_out.astype(bf16)
+    slope_reduce_bias = row_total(reduce_low)
+    slope_reduce = outer_sum(reduce_low, gated_low)
+    grad_hidden = gate_back(linear(reduce_low, w_reduce))[0]
+    hidden_low = grad_hidden.astype(bf16)
+    slope_expand_bias = row_total(hidden_low)
+    slope_expand = outer_sum(normed_three, hidden_low)
+    grad_norm_in, slope_gain_three, slope_bias_three = norm_back_three(linear_back(hidden_low, w_expand))
+    grad_cross = grad_out + grad_norm_in
+    cross_low = grad_cross.astype(bf16)
+    slope_xmixer_bias = row_total(cross_low)
+    slope_xmixer = outer_sum(cross_out, cross_low)
+    grad_heard = linear_back(cross_low, x_mixer).astype(bf16)
+    grad_cq, part_ck, part_cv = attend_back(
+        grad_heard, cross_query, cross_keys_all, cross_values_all, cross_mask, cross_logsum
+    )
+    slope_xkey = outer_sum(frames_all, part_ck.astype(bf16))
+    slope_xvalue = outer_sum(frames_all, part_cv.astype(bf16))
+    slope_xvalue_bias = row_total(part_cv)
+    low_cq = (grad_cq * factor).astype(bf16)
+    slope_xquery_bias = row_total(low_cq)
+    slope_xquery = outer_sum(normed_two, low_cq)
+    grad_norm_two, slope_gain_two, slope_bias_two = norm_back_two(linear_back(low_cq, x_query))
+    grad_self = grad_cross + grad_norm_two
+    self_low = grad_self.astype(bf16)
+    slope_mixer_bias = row_total(self_low)
+    slope_mixer = outer_sum(self_out, self_low)
+    grad_mixed = linear_back(self_low, w_mixer).astype(bf16)
+    grad_q, part_k, part_v = attend_back(grad_mixed, query_low, key_all, value_all, self_mask, self_logsum)
+    low_k, low_v = (
+        lax.psum_scatter(part_k.astype(bf16), "seq", scatter_dimension=1, tiled=True),
+        lax.psum_scatter(part_v.astype(bf16), "seq", scatter_dimension=1, tiled=True),
+    )
+    low_q = (grad_q * factor).astype(bf16)
+    slope_query = outer_sum(normed_one, low_q)
+    slope_query_bias = row_total(low_q)
+    slope_key = outer_sum(normed_one, low_k)
+    slope_value = outer_sum(normed_one, low_v)
+    slope_value_bias = row_total(low_v)
+    grad_normed = linear_back(low_q, w_query) + linear_back(low_k, w_key) + linear_back(low_v, w_value)
+    grad_norm_one, slope_gain_one, slope_bias_one = norm_back_one(grad_normed)
+    tokens_gradient = (grad_self + grad_norm_one).astype(bf16)
+
+    slopes = [
+        slope_query, slope_key, slope_value, slope_xquery, slope_xkey, slope_xvalue, slope_mixer, slope_xmixer
+    ]
+    slopes = [s.astype(bf16).reshape(768, NY, NC, 192) for s in slopes]
+    pair_grads = jnp.stack([
+        jnp.stack([slopes[2 * p], slopes[2 * p + 1]], axis=3).transpose(1, 0, 2, 3, 4).reshape(NY, NZ, NX, 96, 768)
+        for p in range(4)
+    ])
+    wide_grads = slope_expand.astype(bf16).reshape(NZ, NX, 96, 3072)
+    tall_grads = slope_reduce.astype(bf16).reshape(NY, NC, 192, 3072)
+    small_grads = [
+        slope_gain_one, slope_bias_one, slope_query_bias, slope_value_bias, slope_mixer_bias, slope_gain_two,
+        slope_bias_two, slope_xquery_bias, slope_xvalue_bias, slope_xmixer_bias, slope_gain_three,
+        slope_bias_three, slope_expand_bias, slope_reduce_bias,
+    ]
+    small_flat = jnp.concatenate([v.reshape(8, -1) for v in small_grads], axis=1)
+    small_flat = jnp.pad(small_flat, ((0, 0), (0, 2048 - sum(sizes)))).reshape(8, 16, 128)
+    total, small_total = reduce_everything(pair_grads, wide_grads, tall_grads, small_flat)
+    matrices = []
+    for p in range(4):
+        matrices += [total[p, :, :192], total[p, :, 192:]]
+    expand_grad = jnp.concatenate([total[4], total[5]], axis=1)
+    reduce_grad = jnp.concatenate([total[6], total[7]], axis=0).T
+    flat_total = small_total.reshape(-1)
+    smaller, at = [], 0
+    for size in sizes:
+        smaller.append(flat_total[at:at + size])
+        at += size
+    m_query, m_key, m_value, m_xquery, m_xkey, m_xvalue, m_mixer, m_xmixer = matrices
+    return (
+        layer_output, tokens_gradient, smaller[0], smaller[1], m_query, smaller[2], m_key, m_value, smaller[3],
+        m_mixer, smaller[4], smaller[5], smaller[6], m_xquery, smaller[7], m_xkey, m_xvalue, smaller[8],
+        m_xmixer, smaller[9], smaller[10], smaller[11], expand_grad, smaller[12], reduce_grad, smaller[13],
+    )
+
+
 def solution(mesh):
     placed = (
         P("grp", "seq", None),
@@ -407,8 +1020,9 @@
         P("grp", "seq"),
         P("grp"),
     )
+    small_slice = mesh.shape["grp"] == NZ * NX and mesh.shape["seq"] == NY * NC
     return jax.shard_map(
-        on_device,
+        on_device_fast if small_slice else on_device_plain,
         mesh=mesh,
         in_specs=placed,
         out_specs=(

time: 1720 us -> 728 us (0.42)
  waiting for transfers between devices: 1110 us -> 0.04 us
  blocking collectives: 296 us -> 0 us
  Pallas kernels: 0 us -> 212 us
  local copies, waits for them, and re-layouts: 71.7 us -> 251 us
  other arithmetic: 41.8 us -> 86 us
  matrix products: 170 us -> 149 us
    reduce_scatter x13 -> x2, waiting for transfers between devices: 775 us -> 0.01 us  [the longest x1 0.01 us: on_device_fast(): lax.psum_scatter(part_k.astype(bf16), 'seq', scatter_dimension=1, tiled=T...]
    unnamed x46 -> x2, waiting for transfers between devices: 242 us -> 0.03 us
    all_gather x9 -> x0, blocking collectives: 224 us -> none  [the longest x1 26.5 us: on_device(): lax.all_gather(key_weight, 'grp', axis=0, tiled=True)]
    pallas_call x0 -> x2, Pallas kernels: none -> 212 us  [the longest x1 121 us: gather_everything(): pl.pallas_call(gather_kernel, out_shape=(jax.ShapeDtypeStruct((4, NY, NZ,...]
    all_gather x15 -> x0, waiting for transfers between devices: 93.1 us -> none  [the longest x1 33.7 us: on_device(): lax.all_gather(row_parts[9], 'seq', axis=1, tiled=True)]
    another operation x0 -> x12, local copies, waits for them, and re-layouts: none -> 92.6 us  [the longest x8 61.7 us: on_device_fast(): jnp.stack([slopes[2 * p], slopes[2 * p + 1]], axis=3)]
    slice x0 -> x11, local copies, waits for them, and re-layouts: none -> 84.3 us  [the longest x9 83.1 us: on_device_fast(): pairs_all[p, :, :, :, h].transpose(1, 0, 2, 3).reshape(768, 768)]
    unnamed x2 -> x0, blocking collectives: 58.3 us -> none
  transfers between devices with their start and end apart: 37 -> 2, of which waited for: 22 -> 0; matrix products, arithmetic and copies ran while one was open for 12% -> 21% of each run, Pallas kernels for 0% -> 0%
where the time goes in v1:
time: 728 us; the launch traced here: 714 us
  local copies, waits for them, and re-layouts  251 us (34%)
  Pallas kernels  212 us (29%)
  matrix products  149 us (20%)
  other arithmetic  86 us (12%)
  between operations  16 us (2%)
    pallas_call x1, Pallas kernels, gather_everything(): pl.pallas_call(gather_kernel, out_shape=(jax.ShapeDtypeStruct((4, NY, NZ,...  121 us
    pallas_call x1, Pallas kernels, reduce_everything(): pl.pallas_call(reduce_kernel, out_shape=(jax.ShapeDtypeStruct((GROUPS,) +...  90.7 us
    slice x9, local copies, waits for them, and re-layouts, on_device_fast(): pairs_all[p, :, :, :, h].transpose(1, 0, 2, 3).reshape(768, 768)  83.1 us
    another operation x8, local copies, waits for them, and re-layouts, on_device_fast(): jnp.stack([slopes[2 * p], slopes[2 * p + 1]], axis=3)  61.7 us
    transpose x4, other arithmetic, on_device_fast(): jnp.stack([slopes[2 * p], slopes[2 * p + 1]], axis=3)  39.4 us
    dot_general x10, matrix products, linear(): jnp.einsum('bri,ij->brj', inputs, weight, preferred_element_type=jnp.floa...  39.1 us
    dot_general x10, matrix products, outer_sum(): jnp.einsum('bri,brj->ij', inputs, gradient, preferred_element_type=jnp.fl...  34.3 us
    another operation x4, local copies, waits for them, and re-layouts, on_device_fast(): jnp.stack([jnp.stack([slopes[2 * p], slopes[2 * p + 1]], axis=3).transpos...  30.9 us
  transfers between devices with their start and end apart: 2, of which 0 were waited for; matrix products, arithmetic and copies ran while one was open for 21% of the time, Pallas kernels for 0%

profile of v1, /device:TPU:1, one launch (start us, length us, event | category | flops | bytes accessed | tf_op | source)
XLA Modules:
  0.0 713.8 jit_solution(13955989775225970106)
XLA Ops:
  7.9 9.5 %concatenate.28 = bf16[1632]{0:T(1024)(128)(2,1)S(1)} concatenate(bf16[96]{0:T(256)(128)(2,1)} %param.38, bf16[96]{0:T(256)(128)(2,1)} %param.39, bf16[96]{0:T(256)(128)(2,1)} %param.41, bf16[96]{0:T(256)(128)(2,1)} %param.44, bf16[96]{0:T(256)(128)(2,1)} %param.46, bf16[96]{0:T(256)(128)(2,1)} %param.47, bf16[96]{0:T(256)(128)(2,1)} %param.48, bf16[96]{0:T(256)(128)(2,1)} %param.50, ...), dimensions={0} | concatenate | bytes 6528 | tf_op jit(solution)/shard_map/concatenate | solution.py:843
  22.6 121.2 %gather_all.1 = (bf16[4,2,4,2,96,768]{5,4,3,2,1,0:T(8,128)(2,1)}, bf16[4,2,96,3072]{3,2,1,0:T(8,128)(2,1)}, bf16[2,2,192,3072]{3,2,1,0:T(8,128)(2,1)}, bf16[8,16...) custom-call(bf16[4,96,384]{2,1,0:T(8,128)(2,1)} %pad_maximum_fusion.1.pairs_in, ...), custom_call_target="tpu_custom_call" | custom-call | tf_op jit(solution)/shard_map/gather_all/pallas_call | solution.py:624
  152.2 30.8 %reshape.635 = bf16[4,2,768,2,2,192]{5,4,3,2,1,0:T(2,128)(2,1)} reshape(bf16[4,2,4,2,96,768]{5,4,3,2,1,0:T(8,128)(2,1)} %get-tuple-element.36) | data formatting | bytes 18874368 | tf_op jit(solution)/shard_map/reshape | solution.py:854
  183.0 26.9 %fusion.80 = (bf16[1,2,768,2,1,192]{5,4,3,2,1,0:T(2,128)(2,1)}, bf16[1,2,768,2,1,192]{5,4,3,2,1,0:T(2,128)(2,1)}, bf16[1,2,768,2,1,192]{5,4,3,2,1,0:T(2,128)(2,1...) fusion(bf16[4,2,768,2,2,192]{5,4,3,2,1,0:T(2,128)(2,1)} %reshap, ...), kind=kLoop, calls=%fused_computation.211 | loop fusion | bytes 18874368 | tf_op jit(solution)/shard_map/slice | solution.py:856
  259.4 8.1 %copy.158 = bf16[1,2,768,2,1,192]{2,5,4,3,1,0:T(8,128)(2,1)} copy(bf16[1,2,768,2,1,192]{5,4,3,2,1,0:T(2,128)(2,1)} %get-tuple-element.62) | data formatting | bytes 2359296 | tf_op jit(solution)/shard_map/slice | solution.py:856
  279.1 8.1 %copy.162 = bf16[1,2,768,2,1,192]{2,5,4,3,1,0:T(8,128)(2,1)} copy(bf16[1,2,768,2,1,192]{5,4,3,2,1,0:T(2,128)(2,1)} %get-tuple-element.60) | data formatting | bytes 2359296 | tf_op jit(solution)/shard_map/slice | solution.py:856
  299.9 10.6 %add_convert_fusion = bf16[2,1536,768]{1,2,0:T(8,128)(2,1)} fusion(bf16[2,1536,768]{2,1,0:T(8,128)(2,1)} %bitcast.298, bf16[768,768,1]{0,1,2:T(8,128)(2,1)S(1)} %bitcast.332, f32[768]{0:T(1024)S(1)} %copy-done.109), kind=kOutput, calls=%fused_computation.13 | convolution fusion | flops 3628597248 | bytes 10619904 | tf_op jit(solution)/shard_map/bri,ij->brj/dot_general | solution.py:29
  345.6 12.9 %multiply_reduce_fusion = (f32[2,12,112]{2,1,0:T(8,128)S(1)}, f32[2,12,112,1536]{3,2,1,0:T(8,128)}) fusion(f32[2,12,112,1536]{3,2,1,0:T(8,128)} %copy-done, f32[2,12,112]{2,1,0:T(8,128)S(1)} %log_add_fusion.1, pred[2,1536]{1,0:T(4,128)(4,1)S(1)} %compare_and_fusion, bf16[2,112,12,64]{1,3,2,0:T(8,128)(2,1)S(1)} %bitcast.314, ...), kind=kOutput, calls=%fused_computation.1 | convolution fusion | flops 544994688 | bytes 38117376 | tf_op jit(solution)/shard_map/bqhd,bkhd->bhqk/dot_general | solution.py:74
  358.5 12.0 %multiply_convert_fusion = bf16[2,12,112,1536]{3,2,1,0:T(8,128)(2,1)S(1)} fusion(f32[2,12,112,1536]{3,2,1,0:T(8,128)} %get-tuple-element.118, f32[2,12,112,1536]{3,2,1,0:T(8,128)} %copy-done, f32[2,12,112]{2,1,0:T(8,128)S(1)} %get-tuple-element.117, f32[2,12,112]{2,1,0:T(8,128)S(1)} %log_add_fusion.1, pred[2,1536]{1,0:T(4,128)(4,1)S(1)} %compare_and_fusion), kind=kLoop, calls=%fused_computation | loop fusion | flops 20643840 | bytes 41312256 | tf_op jit(solution)/shard_map/convert_element_type | solution.py:78
  403.4 11.6 %bitcast_convert_fusion.2 = (bf16[2,1536,12,64]{1,3,2,0:T(8,128)(2,1)}, f32[2,12,64,1536]{3,2,1,0:T(8,128)}) fusion(bf16[2,112,12,64]{1,3,2,0:T(8,128)(2,1)S(1)} %bitcast.315, f32[2,12,112,1536]{3,2,1,0:T(8,128)} %copy-done, f32[2,12,112]{2,1,0:T(8,128)S(1)} %copy-done.45, pred[2,1536]{1,0:T(4,128)(4,1)S(1)} %copy-done.42), kind=kOutput, calls=%fused_computation.12 | convolution fusion | flops 543227904 | bytes 31028736 | tf_op jit(solution)/shard_map/bhqk,bqhd->bkhd/dot_general | solution.py:85
  429.9 9.9 %maximum_bitcast_fusion.3 = bf16[2,768,2,2,192]{4,3,2,1,0:T(2,128)(2,1)} fusion(bf16[768,2,2,1,192]{4,3,2,0,1:T(2,128)(2,1)} %copy.189, bf16[768,2,2,1,192]{4,3,2,0,1:T(2,128)(2,1)} %copy.188), kind=kLoop, calls=%fused_computation.33 | loop fusion | flops 4718592 | bytes 4718592 | tf_op jit(solution)/shard_map/transpose | solution.py:958
  446.9 8.6 %bitcast_convert_fusion.5 = bf16[768,768]{0,1:T(8,128)(2,1)} fusion(bf16[2,1536,768]{1,2,0:T(8,128)(2,1)} %bitcast.311, bf16[2,1536,768]{2,1,0:T(8,128)(2,1)} %bitcast.299), kind=kOutput, calls=%fused_computation.54 | convolution fusion | flops 3624468480 | bytes 10616832 | tf_op jit(solution)/shard_map/bri,brj->ij/dot_general | solution.py:37
  455.5 8.7 %copy.185 = bf16[768,2,2,1,192]{4,3,2,0,1:T(2,128)(2,1)} copy(bf16[768,2,2,1,192]{0,4,2,1,3:T(8,128)(2,1)} %bitcast.336) | data formatting | bytes 2359296 | tf_op jit(solution)/shard_map/stack;reshape | solution.py:958
  464.3 8.6 %bitcast_convert_fusion.6 = bf16[768,768]{0,1:T(8,128)(2,1)} fusion(bf16[2,1536,768]{1,2,0:T(8,128)(2,1)} %bitcast.296, bf16[2,1536,768]{2,1,0:T(8,128)(2,1)} %bitcast.300), kind=kOutput, calls=%fused_computation.55 | convolution fusion | flops 3624468480 | bytes 10616832 | tf_op jit(solution)/shard_map/bri,brj->ij/dot_general | solution.py:37
  472.9 8.3 %copy.184 = bf16[768,2,2,1,192]{4,3,2,0,1:T(2,128)(2,1)} copy(bf16[768,2,2,1,192]{0,4,2,1,3:T(8,128)(2,1)} %bitcast.333) | data formatting | bytes 2359296 | tf_op jit(solution)/shard_map/stack;reshape | solution.py:958
  481.2 9.8 %maximum_bitcast_fusion.2 = bf16[2,768,2,2,192]{4,3,2,1,0:T(2,128)(2,1)} fusion(bf16[768,2,2,1,192]{4,3,2,0,1:T(2,128)(2,1)} %copy.185, bf16[768,2,2,1,192]{4,3,2,0,1:T(2,128)(2,1)} %copy.184), kind=kLoop, calls=%fused_computation.32 | loop fusion | flops 4718592 | bytes 4718592 | tf_op jit(solution)/shard_map/transpose | solution.py:958
  501.7 8.3 %copy.183 = bf16[768,2,2,1,192]{4,3,2,0,1:T(2,128)(2,1)} copy(bf16[768,2,2,1,192]{0,4,2,1,3:T(8,128)(2,1)} %bitcast.310) | data formatting | bytes 2359296 | tf_op jit(solution)/shard_map/stack;reshape | solution.py:958
  511.7 8.5 %copy.179 = bf16[768,2,2,1,192]{4,3,2,0,1:T(2,128)(2,1)} copy(bf16[768,2,2,1,192]{0,4,2,1,3:T(8,128)(2,1)} %bitcast.337) | data formatting | bytes 2359296 | tf_op jit(solution)/shard_map/stack;reshape | solution.py:958
  544.5 8.3 %copy.182 = bf16[768,2,2,1,192]{4,3,2,0,1:T(2,128)(2,1)} copy(bf16[768,2,2,1,192]{0,4,2,1,3:T(8,128)(2,1)} %bitcast.338) | data formatting | bytes 2359296 | tf_op jit(solution)/shard_map/stack;reshape | solution.py:958
  552.8 9.8 %maximum_bitcast_fusion.1 = bf16[2,768,2,2,192]{4,3,2,1,0:T(2,128)(2,1)} fusion(bf16[768,2,2,1,192]{4,3,2,0,1:T(2,128)(2,1)} %copy.183, bf16[768,2,2,1,192]{4,3,2,0,1:T(2,128)(2,1)} %copy.182), kind=kLoop, calls=%fused_computation.31 | loop fusion | flops 4718592 | bytes 4718592 | tf_op jit(solution)/shard_map/transpose | solution.py:958
  573.2 8.3 %copy.180 = bf16[768,2,2,1,192]{4,3,2,0,1:T(2,128)(2,1)} copy(bf16[768,2,2,1,192]{0,4,2,1,3:T(8,128)(2,1)} %bitcast.334) | data formatting | bytes 2359296 | tf_op jit(solution)/shard_map/stack;reshape | solution.py:958
  581.5 9.8 %maximum_bitcast_fusion = bf16[2,768,2,2,192]{4,3,2,1,0:T(2,128)(2,1)} fusion(bf16[768,2,2,1,192]{4,3,2,0,1:T(2,128)(2,1)} %copy.180, bf16[768,2,2,1,192]{4,3,2,0,1:T(2,128)(2,1)} %copy.179), kind=kLoop, calls=%fused_computation.30 | loop fusion | flops 4718592 | bytes 4718592 | tf_op jit(solution)/shard_map/transpose | solution.py:958
  591.3 8.1 %stack_reshape.38 = bf16[1,2,4,2,96,768]{5,4,3,2,1,0:T(8,128)(2,1)} reshape(bf16[2,768,2,2,192]{4,3,2,1,0:T(2,128)(2,1)} %maximum_bitcast_fusion) | data formatting | bytes 4718592 | tf_op jit(solution)/shard_map/stack;reshape | solution.py:957
  608.9 90.7 %reduce_all.1 = (f32[8,96,384]{2,1,0:T(8,128)}, f32[16,128]{1,0:T(8,128)}) custom-call(bf16[4,2,4,2,96,768]{5,4,3,2,1,0:T(8,128)(2,1)} %pad_maximum_fusion.pairs, bf16[4,2,96,3072]{3,2,1,0:T(8,128)(2,1)} %bitcast.279, bf16[2,2,192,3072]{3,2,1,0:T(8,128)(2,1)} %bitcast.278, f32[8,16,128]{2,1,0:T(8,128)} %bitcast.339), custom_call_target="tpu_custom_call" | custom-call | tf_op jit(solution)/shard_map/reduce_all/pallas_call | solution.py:795
  (411 shorter events, 240.2 us)
Async XLA Ops:
  7.2 14.4 %copy-start.56 = (bf16[96,192]{1,0:T(8,128)(2,1)S(1)}, bf16[96,192]{1,0:T(8,128)(2,1)}, u32[]{:S(2)}) copy-start(bf16[96,192]{1,0:T(8,128)(2,1)} %param.52) | copy-start | bytes 110596
  7.2 14.4 %copy-start.57 = (bf16[96,192]{1,0:T(8,128)(2,1)S(1)}, bf16[96,192]{1,0:T(8,128)(2,1)}, u32[]{:S(2)}) copy-start(bf16[96,192]{1,0:T(8,128)(2,1)} %param.51) | copy-start | bytes 110596
  7.2 14.4 %copy-start.58 = (bf16[96,192]{1,0:T(8,128)(2,1)S(1)}, bf16[96,192]{1,0:T(8,128)(2,1)}, u32[]{:S(2)}) copy-start(bf16[96,192]{1,0:T(8,128)(2,1)} %param.54) | copy-start | bytes 110596
  7.2 14.4 %copy-start.59 = (bf16[96,192]{1,0:T(8,128)(2,1)S(1)}, bf16[96,192]{1,0:T(8,128)(2,1)}, u32[]{:S(2)}) copy-start(bf16[96,192]{1,0:T(8,128)(2,1)} %param.45) | copy-start | bytes 110596
  7.2 14.5 %copy-start.60 = (bf16[96,192]{1,0:T(8,128)(2,1)S(1)}, bf16[96,192]{1,0:T(8,128)(2,1)}, u32[]{:S(2)}) copy-start(bf16[96,192]{1,0:T(8,128)(2,1)} %param.42) | copy-start | bytes 110596
  7.3 14.5 %copy-start.61 = (bf16[96,192]{1,0:T(8,128)(2,1)S(1)}, bf16[96,192]{1,0:T(8,128)(2,1)}, u32[]{:S(2)}) copy-start(bf16[96,192]{1,0:T(8,128)(2,1)} %param.40) | copy-start | bytes 110596
  7.3 14.5 %copy-start.62 = (bf16[96,192]{1,0:T(8,128)(2,1)S(1)}, bf16[96,192]{1,0:T(8,128)(2,1)}, u32[]{:S(2)}) copy-start(bf16[96,192]{1,0:T(8,128)(2,1)} %param.49) | copy-start | bytes 110596
  7.3 14.5 %copy-start.63 = (bf16[96,192]{1,0:T(8,128)(2,1)S(1)}, bf16[96,192]{1,0:T(8,128)(2,1)}, u32[]{:S(2)}) copy-start(bf16[96,192]{1,0:T(8,128)(2,1)} %param.43) | copy-start | bytes 110596
  7.3 530.7 %reduce-scatter.3.cloned.1.call-start = ((), (), s32[]{:S(2)}) async-start(), calls=%async_computation.2 | async-start | bytes 1720320 | tf_op jit(solution)/shard_map/reduce_scatter | solution.py:940
  146.8 80.6 %copy-start.75 = (f32[768]{0:T(1024)}, f32[768]{0:T(1024)S(1)}, u32[]{:S(2)}) copy-start(f32[768]{0:T(1024)S(1)} %reshape.674) | copy-start | bytes 9220
  146.9 80.5 %copy-start.48 = (f32[768]{0:T(1024)}, f32[768]{0:T(1024)S(1)}, u32[]{:S(2)}) copy-start(f32[768]{0:T(1024)S(1)} %reshape.673) | copy-start | bytes 9220
  228.2 13.4 %copy-start.28 = (bf16[2,112,768]{1,2,0:T(8,128)(2,1)}, bf16[2,112,768]{1,2,0:T(8,128)(2,1)S(1)}, u32[]{:S(2)}) copy-start(bf16[2,112,768]{1,2,0:T(8,128)(2,1)S(1)} %copy.150) | copy-start | bytes 1032196
  244.4 134.6 %copy-start.43 = (f32[2,12,112]{2,1,0:T(8,128)}, f32[2,12,112]{2,1,0:T(8,128)S(1)}, u32[]{:S(2)}) copy-start(f32[2,12,112]{2,1,0:T(8,128)S(1)} %log_add_fusion) | copy-start | bytes 32260
  294.0 64.5 %copy-start.41 = (pred[2,1536]{1,0:T(4,128)(4,1)}, pred[2,1536]{1,0:T(4,128)(4,1)S(1)}, u32[]{:S(2)}) copy-start(pred[2,1536]{1,0:T(4,128)(4,1)S(1)} %compare_and_fusion) | copy-start | bytes 9220
  296.5 14.0 %copy-start = (f32[2,12,112,1536]{3,2,1,0:T(8,128)}, f32[2,12,112,1536]{3,2,1,0:T(8,128)S(1)}, u32[]{:S(2)}) copy-start(f32[2,12,112,1536]{3,2,1,0:T(8,128)S(1)} %get-tuple-element.111) | copy-start | bytes 49545220
  299.8 58.7 %copy-start.44 = (f32[2,12,112]{2,1,0:T(8,128)}, f32[2,12,112]{2,1,0:T(8,128)S(1)}, u32[]{:S(2)}) copy-start(f32[2,12,112]{2,1,0:T(8,128)S(1)} %log_add_fusion.1) | copy-start | bytes 32260
  325.2 15.2 %copy-start.46 = (f32[768]{0:T(1024)}, f32[768]{0:T(1024)S(1)}, u32[]{:S(2)}) copy-start(f32[768]{0:T(1024)S(1)} %reshape.683) | copy-start | bytes 9220
  326.8 13.6 %copy-start.7 = (f32[2,112,768]{2,1,0:T(8,128)}, f32[2,112,768]{2,1,0:T(8,128)S(1)}, u32[]{:S(2)}) copy-start(f32[2,112,768]{2,1,0:T(8,128)S(1)} %get-tuple-element.113) | copy-start | bytes 2064388
  326.8 13.6 %copy-start.73 = (f32[2,112]{1,0:T(2,128)}, f32[2,112]{1,0:T(2,128)S(1)}, u32[]{:S(2)}) copy-start(f32[2,112]{1,0:T(2,128)S(1)} %broadcast_multiply_fusion.1) | copy-start | bytes 2692
  327.1 13.4 %copy-start.93 = (f32[2,112]{1,0:T(2,128)}, f32[2,112]{1,0:T(2,128)S(1)}, u32[]{:S(2)}) copy-start(f32[2,112]{1,0:T(2,128)S(1)} %fusion.65) | copy-start | bytes 2692
  327.4 13.4 %copy-start.70 = (f32[2,112]{1,0:T(2,128)}, f32[2,112]{1,0:T(2,128)S(1)}, u32[]{:S(2)}) copy-start(f32[2,112]{1,0:T(2,128)S(1)} %compare_select_fusion.1) | copy-start | bytes 2692
  340.8 17.7 %copy-start.104 = (f32[2,112]{1,0:T(2,128)}, f32[2,112]{1,0:T(2,128)S(1)}, u32[]{:S(2)}) copy-start(f32[2,112]{1,0:T(2,128)S(1)} %negate_multiply_fusion.2) | copy-start | bytes 2692
  345.6 24.9 %slice-start.4 = ((s8[4718592]{0:T(1024)(128)(4,1)}), s8[4194304]{0:T(1024)(128)(4,1)S(1)}, s32[]{:S(2)}) async-start(s8[4718592]{0:T(1024)(128)(4,1)} %bitcast.281), calls=%async_computation.8 | async-start | bytes 8388608
  390.6 150.0 %reduce-scatter.5.cloned.1.call-start = ((), (), s32[]{:S(2)}) async-start(), calls=%async_computation.3 | async-start | bytes 1720320 | tf_op jit(solution)/shard_map/reduce_scatter | solution.py:941
  (105 other events, 613.9 us)
Sparse Core Ops, SparseCore 0:
  390.7 23.6 reduce-scatter.2
  417.1 26.9 reduce-scatter.4
